TPU v7x, 256 devices: a whole 4x4x8 slice. The times are simulated.
256 devices in a mesh: fx: 8 (over z), fy: 16 (over x, y), grp: 2 (over core).
Axes of the slice: x: 4, y: 4, z: 8, core: 2. Of those that a mesh axis runs over, the one named last changes fastest.
Arguments:
- efield: float32 [3, 32, 128, 4096], P(None, None, 'fx', ('fy', 'grp')), may hold values from -6 to 6
- hfield: float32 [3, 32, 128, 4096], P(None, None, 'fx', ('fy', 'grp')), may hold values from -6 to 6
- loss_coef: float32 [32, 128, 4096], P(None, 'fx', ('fy', 'grp')), may hold values from 0.8 to 1
- update_coef: float32 [32, 128, 4096], P(None, 'fx', ('fy', 'grp')), may hold values from 0.2 to 0.6
- port_count: int32 [256], replicated, may hold values from 1 to 32, 4096 in all
- port_perm: int32 [4096], replicated, may hold values from 0 to 4095, each once
- port_cell: int32 [256, 32], P(('fx', 'fy', 'grp')), may hold values from 0 to 2047
- pole_state: float32 [2048, 256], P(('fx', 'fy', 'grp')), may hold values from -6 to 6
- transition: float32 [2048, 256, 256], P(('fx', 'fy', 'grp')), may hold values from -0.25 to 0.25
- input_map: float32 [2048, 256, 2], P(('fx', 'fy', 'grp')), may hold values from -6 to 6
- output_map: float32 [2048, 2, 256], P(('fx', 'fy', 'grp')), may hold values from -0.375 to 0.375
- feedthrough: float32 [2048, 2, 2], P(('fx', 'fy', 'grp')), may hold values from -4 to 4
Outputs:
- efield_out: float32 [3, 32, 128, 4096], P(None, None, 'fx', ('fy', 'grp'))
- hfield_out: float32 [3, 32, 128, 4096], P(None, None, 'fx', ('fy', 'grp'))
- final_state: float32 [2048, 256], P(('fx', 'fy', 'grp'))
Inputs may be any that keep to these rules, and one draw needn't show every extreme that they name: `port_count`: each tile holds between 1 and 32 ports, 4096 in all; some tile holds exactly 32. `port_perm`: each live port number once. `port_cell`: cell x * 128 + y within the tile; slots at or beyond the tile's port_count are unused.
All inputs are finite; a program needn't handle non-finite values.
Results may differ from a plain program's by a relative error of at most 0.0003.
Values sent between devices are 32-bit elements; how exact they have to be, the bound alone decides.
No kernel may reach another device: no remote copies, remote signals or barrier semaphores. Data moves between devices by JAX's collectives and lax.ppermute only.
A program may use at most 64 MiB of HBM per device.

v0:
```python
import functools

import jax
import jax.numpy as jnp
from jax import lax
from jax.experimental import pallas as pl
from jax.experimental.pallas import tpu as pltpu
from jax.sharding import PartitionSpec as P

K = 4
BLOCKS = 2
COURANT = 0.5
HIGH = lax.Precision.HIGHEST
ALL = ("fx", "fy", "grp")
Z, X, Y = 32, 16, 128
SLOTS = 32
LIST = 9 * SLOTS
MODELS = 8
F32 = jnp.float32
I32 = jnp.int32
LANE_O, LANE_D, LANE_C = 32, 48, 80
OWN, MATE, DRAWN, SELF, CROSS, CELL, MASKS = 0, 288, 592, 880, 1168, 1456, 1744
STRIP = 16 * Z
LAG_E, LAG_H = 6, 4


def iota(shape, dim):
    return lax.broadcasted_iota(I32, shape, dim)


class Copies:
    def __init__(self, sems):
        self.sems, self.used, self.open = sems, 0, []

    def start(self, source, target):
        copy = pltpu.make_async_copy(source, target, self.sems.at[self.used])
        self.used += 1
        copy.start()
        self.open.append(copy)

    def group(self):
        group, self.open = self.open, []
        return group

    def wait(self, group=None):
        for copy in self.group() if group is None else group:
            copy.wait()


def port_means(mean, cells):
    pick_y = (iota((Y, SLOTS), 0) == cells % Y).astype(F32)
    columns = jnp.dot(mean, pick_y, precision=HIGH, preferred_element_type=F32)
    return jnp.sum(jnp.where(iota((X, SLOTS), 0) == cells // Y, columns, 0.0), axis=0, keepdims=True)


def drawn_lanes(output_ref, state):
    lane, model = iota((MODELS, Y), 1), iota((MODELS, Y), 0)
    row = jnp.zeros((1, Y), F32)
    for q in range(2):
        drawn = jnp.sum(output_ref[:, q, :] * state, axis=1, keepdims=True)
        row = row + jnp.sum(
            jnp.where(lane == LANE_O + 2 * model + q, drawn, 0.0), axis=0, keepdims=True
        )
    return row


def pack_rows(read, up_ref, down_ref, c):
    low = iota((8, Y), 0) < 4
    for z in range(Z // 2):
        a, b = read(z), read(z + Z // 2)
        up_ref[16 * c + z] = jnp.where(low, a[:8], pltpu.roll(b[:8], 4, 0))
        down_ref[16 * c + z] = jnp.where(low, pltpu.roll(b[8:], 4, 0), a[8:])


def load_parts(copies, e_hbm, h_hbm, loss_hbm, gain_hbm, parts):
    sources = [e_hbm.at[c] for c in range(3)] + [h_hbm.at[c] for c in range(3)] + [loss_hbm, gain_hbm]
    groups = []
    for c, source in enumerate(sources):
        copies.start(source, parts.at[c])
        groups.append(copies.group())
    return groups


def first_kernel(
    e_hbm, h_hbm, loss_hbm, gain_hbm, feed_hbm, cells_hbm, state_hbm, output_hbm,
    even_out, odd_out, row_out, fixed_out,
    parts, feed, cells, state, output, sent, line, row, fixed, sems,
):
    copies = Copies(sems)
    groups = load_parts(copies, e_hbm, h_hbm, loss_hbm, gain_hbm, parts)
    for origin, target in ((feed_hbm, feed), (cells_hbm, cells), (state_hbm, state), (output_hbm, output)):
        copies.start(origin, target)
    small = copies.group()
    odd = lax.axis_index("fx") % 2
    for c in range(8):
        copies.wait(groups[c])
        pack_rows(lambda z: parts[c, z], sent.at[1 - odd], sent.at[odd], c)
        own = pl.ds(16 * c, 16)
        copies.start(sent.at[0, own], even_out.at[own])
        copies.start(sent.at[1, own], odd_out.at[own])
    copies.wait(small)
    mean = parts[2, 0]
    for z in range(1, Z):
        mean = mean + parts[2, z]
    line[...] = jnp.zeros_like(line)
    line[0:1, :SLOTS] = cells[...].astype(F32)
    for k in range(4):
        line[k + 1 : k + 2, :MODELS] = feed[k // 2, k % 2 : k % 2 + 1, :]
    lines = line[...]
    total = pltpu.roll(lines, LANE_C, 1)[0:1]
    for k in range(4):
        total = total + pltpu.roll(lines, LANE_D + 8 * k, 1)[k + 1 : k + 2]
    fixed[...] = total
    row[...] = jnp.broadcast_to(total + drawn_lanes(output, state[...]), row.shape)
    row[:, :SLOTS] = jnp.broadcast_to(port_means(mean * (1.0 / Z), cells[...]), (256, SLOTS))
    copies.start(row, row_out)
    copies.start(fixed, fixed_out)
    copies.wait()


def side_kernel(
    e_hbm, h_hbm, loss_hbm, gain_hbm, even_hbm, odd_hbm, halo_out, pack_out, even_out, odd_out,
    parts, got, halo, pack, sent, sems,
):
    copies = Copies(sems)
    groups = []
    sources = [e_hbm.at[c] for c in range(3)] + [h_hbm.at[c] for c in range(3)] + [loss_hbm, gain_hbm]
    for c, source in enumerate(sources):
        own = pl.ds(16 * c, 16)
        copies.start(even_hbm.at[own], got.at[0, own])
        copies.start(odd_hbm.at[own], got.at[1, own])
        copies.start(source, parts.at[c])
        groups.append(copies.group())
    odd = lax.axis_index("fx") % 2
    after, before = got.at[odd], got.at[1 - odd]
    odd = lax.axis_index(("fy", "grp")) % 2
    to_right, to_left = sent.at[odd], sent.at[1 - odd]
    low = iota((8, Y), 0) < 4
    group = iota((8, Y), 1) // 16
    half = iota((8, Y), 1) % 16 < 8
    for c in range(8):
        copies.wait(groups[c])
        for z in range(Z // 2):
            a, b = after[16 * c + z], before[16 * c + z]
            halo[c, z] = jnp.where(low, a, b)
            halo[c, z + Z // 2] = pltpu.roll(jnp.where(low, b, a), 4, 0)
        totals = []
        for part in range(4):
            total = [jnp.zeros((8, Y), F32)] * 3
            for zl in range(8):
                z = part * 8 + zl
                plane = parts[c, z]
                for i, tile in enumerate((plane[:8], plane[8:], halo[c, z])):
                    moved = pltpu.roll(tile, (16 * zl + 8) % Y, 1)
                    total[i] = jnp.where(group == zl, moved, total[i])
            totals.append(total)
            for i in range(3):
                pack[c, 8 * i : 8 * i + 8, Y * part : Y * part + Y] = total[i]
        for pair in range(2):
            for i in range(3):
                a, b = totals[2 * pair][i], totals[2 * pair + 1][i]
                rows, lanes = slice(8 * i, 8 * i + 8), slice(Y * pair, Y * pair + Y)
                to_right[c, rows, lanes] = jnp.where(half, a, pltpu.roll(b, 8, 1))
                to_left[c, rows, lanes] = jnp.where(half, pltpu.roll(a, Y - 8, 1), b)
        copies.start(pack.at[c], pack_out.at[c])
        copies.start(sent.at[0, c], even_out.at[c])
        copies.start(sent.at[1, c], odd_out.at[c])
        copies.start(halo.at[c], halo_out.at[c])
    copies.wait()


def index_kernel(
    counts_hbm, perm_hbm, gathered_hbm, moved_hbm, inputs_hbm, output_hbm, fixed_hbm,
    pick_out, mask_out, source_out, state_out, line_out,
    counts_ref, perm_ref, gathered, moved, inputs, output, fixed, pick, mask, source, new_state, line, sems,
):
    copies = Copies(sems)
    copies.start(counts_hbm, counts_ref)
    copies.start(perm_hbm, perm_ref)
    early = copies.group()
    pairs = ((gathered_hbm, gathered), (moved_hbm, moved), (inputs_hbm, inputs), (output_hbm, output), (fixed_hbm, fixed))
    for origin, target in pairs:
        copies.start(origin, target)
    late = copies.group()
    copies.wait(early)
    me, fx, fy = lax.axis_index(ALL), lax.axis_index("fx"), lax.axis_index(("fy", "grp"))
    counts = counts_ref[...]
    starts = counts
    for width in (1, 2, 4, 8, 16, 32, 64, 128):
        starts = starts + jnp.where(iota((1, 256), 1) >= width, pltpu.roll(starts, width, 1), 0)
    starts = starts - counts
    number = iota((LIST, 1), 0)
    slot = number % SLOTS
    dx, dy = number // SLOTS // 3 - 1, number // SLOTS % 3 - 1
    inside = (fx + dx >= 0) & (fx + dx < 8) & (fy + dy >= 0) & (fy + dy < 32)
    tile = jnp.where(inside, me + 32 * dx + dy, -1)
    own = iota((LIST, 256), 1) == tile
    start = jnp.sum(jnp.where(own, starts, 0), axis=1, keepdims=True)
    count = jnp.sum(jnp.where(own, counts, 0), axis=1, keepdims=True)
    live = slot < count
    wanted = jnp.where(live, start + slot, -1)
    even = iota((32, Y), 1) % 2 == 0
    perm = perm_ref[...]
    mates = jnp.where(even, pltpu.roll(perm, Y - 1, 1), pltpu.roll(perm, 1, 1))
    position = jnp.zeros((LIST, Y), I32)
    partner = jnp.zeros((LIST, Y), I32)
    spot = iota((2 * MODELS, Y), 0)
    mine_at = me * 2 * MODELS + 2 * (spot % MODELS) + spot // MODELS
    mine = jnp.zeros((2 * MODELS, Y), I32)
    for r in range(32):
        row, mate = perm[r : r + 1], mates[r : r + 1]
        hit = row == wanted
        position = jnp.where(hit, iota((LIST, Y), 1) + Y * r, position)
        partner = jnp.where(hit, mate, partner)
        mine = jnp.where(iota((2 * MODELS, Y), 1) + Y * r == mine_at, row, mine)
    position = jnp.sum(position, axis=1, keepdims=True)
    partner = jnp.sum(partner, axis=1, keepdims=True)
    mine = jnp.sum(mine, axis=1, keepdims=True)
    ports = jnp.concatenate([partner, mine], axis=0)
    total = LIST + 2 * MODELS
    before = starts <= ports
    port_tile = jnp.sum(before.astype(I32), axis=1, keepdims=True) - 1
    port_start = jnp.max(jnp.where(before, starts, 0), axis=1, keepdims=True)
    port_slot = ports - port_start
    pick[:LIST] = own.astype(F32).astype(jnp.bfloat16)
    pick[LIST : LIST + total] = (iota((total, 256), 1) == port_tile).astype(F32).astype(jnp.bfloat16)
    pick[LIST + total :] = (iota((LIST, 256), 1) == position // 16).astype(F32).astype(jnp.bfloat16)
    lane = iota((LIST, Y), 1)
    q = position % 2
    model = position // 2 % MODELS
    on = live.astype(F32)
    mask[OWN:MATE] = jnp.where(lane == slot, on, 0.0)
    mask[MATE:DRAWN] = (iota((total, Y), 1) == port_slot).astype(F32)
    mask[DRAWN:SELF] = jnp.where(lane == LANE_O + 2 * model + q, on, 0.0)
    mask[SELF:CROSS] = jnp.where(lane == LANE_D + 24 * q + model, on, 0.0)
    mask[CROSS:CELL] = jnp.where(lane == LANE_D + 8 * (q + 1) + model, on, 0.0)
    mask[CELL:] = (lane == LANE_C + slot).astype(F32)
    copies.start(pick, pick_out)
    copies.start(mask, mask_out)
    copies.wait(late)
    source[...], mine = port_sources(gathered, pick, mask)
    new_state[...] = moved[...] + input_part(inputs, mine)
    line[...] = fixed[...] + drawn_lanes(output, new_state[...])
    copies.start(source, source_out)
    copies.start(new_state, state_out)
    copies.start(line, line_out)
    copies.wait()


def port_sources(gathered_ref, pick_ref, mask_ref):
    gathered = gathered_ref[...]
    high = gathered.astype(jnp.bfloat16)
    left_over = gathered - high.astype(F32)
    middle = left_over.astype(jnp.bfloat16)
    low = (left_over - middle.astype(F32)).astype(jnp.bfloat16)
    picked = jnp.dot(
        pick_ref[...], jnp.concatenate([high, middle, low], axis=1), preferred_element_type=F32
    )
    picked = picked[:, :Y] + picked[:, Y : 2 * Y] + picked[:, 2 * Y :]
    total = LIST + 2 * MODELS

    def choose(part, mask):
        return jnp.sum(part * mask, axis=1, keepdims=True)

    of_tile, of_port, of_model = picked[:LIST], picked[LIST : LIST + total], picked[LIST + total :]
    own = choose(of_tile, mask_ref[OWN:MATE])
    others = choose(of_port, mask_ref[MATE:DRAWN])
    mate, mine = others[:LIST], others[LIST:]
    current = choose(
        of_model, mask_ref[DRAWN:SELF] + mask_ref[SELF:CROSS] * own + mask_ref[CROSS:CELL] * mate
    )
    cell = choose(of_tile, mask_ref[CELL:]).astype(I32)
    number = iota((LIST, 1), 0) // SLOTS
    x = (number // 3 - 1) * X + cell // Y
    y = (number % 3 - 1) * Y + cell % Y
    lane = iota((LIST, 2 * Y), 1)
    lane_y = jnp.where(lane < Y, lane, jnp.where(lane < Y + 16, lane - 136, jnp.where(lane < Y + 32, lane - 24, -1000)))
    row = iota((LIST, Y), 1)
    row_x = jnp.where(row < 20, row, jnp.where(row < 24, row - 24, -1000))
    spread = jnp.where(lane_y == y, current, 0.0)
    to_row = (row_x == x).astype(F32)
    source = lax.dot_general(
        to_row, spread, (((0,), (0,)), ((), ())), precision=HIGH, preferred_element_type=F32
    )[:24]
    return source, mine


def input_part(inputs, mine):
    return inputs[:, 0, :] * mine[:MODELS] + inputs[:, 1, :] * mine[MODELS:]


def repeat_groups(row_lanes):
    value = jnp.where(iota(row_lanes.shape, 1) < 16, row_lanes, 0.0)
    for width in (16, 32, 64):
        value = value + pltpu.roll(value, width, 1)
    return jnp.concatenate([value] * 4, axis=1)


def strip_step(fields, loss, gain, drive, keep_x, z_first, z_last):
    ex, ey, ez, hx, hy, hz = fields

    def up(v):
        return jnp.where(z_last, 0.0, pltpu.roll(v, STRIP - 16, 1))

    def down(v):
        return jnp.where(z_first, 0.0, pltpu.roll(v, 16, 1))

    hx = hx - COURANT * ((pltpu.roll(ez, STRIP - 1, 1) - ez) - (up(ey) - ey))
    hy = (hy - COURANT * ((up(ex) - ex) - (pltpu.roll(ez, 23, 0) - ez))) * keep_x
    hz = (hz - COURANT * ((pltpu.roll(ey, 23, 0) - ey) - (pltpu.roll(ex, STRIP - 1, 1) - ex))) * keep_x
    ex = loss * ex + gain * ((hz - pltpu.roll(hz, 1, 1)) - (hy - down(hy)))
    ey = loss * ey + gain * ((hx - down(hx)) - (hz - pltpu.roll(hz, 1, 0)))
    ez = loss * ez + gain * ((hy - pltpu.roll(hy, 1, 0)) - (hx - pltpu.roll(hx, 1, 1)) - drive)
    return [ex, ey, ez, hx, hy, hz]


def walls():
    keep_x = jnp.where((iota((24, 1), 0) >= 20) & (lax.axis_index("fx") == 0), 0.0, 1.0)
    return keep_x, jnp.where(lax.axis_index(("fy", "grp")) == 0, 0.0, 1.0)


def drives_of(source):
    return repeat_groups(source[:, Y:]), repeat_groups(pltpu.roll(source[:, Y:], Y - 16, 1))


def strips_step(s, strips, edge_coefs, seam, drives):
    keep_x, keep_y = walls()
    lanes = iota((24, STRIP), 1)
    ends = (keep_x, lanes < 16, lanes >= STRIP - 16)
    low_next = strip_step([strips[c] for c in range(6)], edge_coefs[0], edge_coefs[1], drives[0], *ends)
    for i, (e_at, h_at) in enumerate(((2, 3), (0, 5))):
        joined = jnp.where(lanes % 16 == 8, strips[6 + e_at], pltpu.roll(low_next[h_at] * keep_y, 2, 1))
        for part in range(4):
            seam[s, i, part] = joined[:, Y * part : Y * part + Y]
    high_next = strip_step([strips[6 + c] for c in range(6)], edge_coefs[2], edge_coefs[3], drives[1], *ends)
    for c in range(6):
        strips[c] = low_next[c]
        strips[6 + c] = high_next[c]


def sweep(s, state, coef, seam, source):
    keep_x, _ = walls()
    lane = iota((24, Y), 1)
    end, begin = lane == Y - 1, lane == 0

    def turned(z):
        turn = (247 - 16 * (z % 8)) % Y
        return pltpu.roll(seam[s, 0, z // 8], turn, 1), pltpu.roll(seam[s, 1, z // 8], turn, 1)

    def shift_electric(z):
        seam_a, seam_b = turned(z)
        return (
            jnp.where(end, seam_a, pltpu.roll(state[2, z], Y - 1, 1)),
            jnp.where(end, seam_b, pltpu.roll(state[0, z], Y - 1, 1)),
            seam_a,
            seam_b,
        )

    def magnetic(z, ez_next, ex_next, seam_a, seam_b):
        ex, ey, ez = state[0, z], state[1, z], state[2, z]
        hx = state[3, z + 1] - COURANT * ((ez_next - ez) - (state[1, z + 1] - ey))
        hy = state[4, z + 1] - COURANT * ((state[0, z + 1] - ex) - (pltpu.roll(ez, 23, 0) - ez))
        hz = state[5, z + 1] - COURANT * ((pltpu.roll(ey, 23, 0) - ey) - (ex_next - ex))
        hy = hy * keep_x
        hz = hz * keep_x
        state[3, z + 1] = hx
        state[4, z + 1] = hy
        state[5, z + 1] = hz
        return (
            jnp.where(begin, seam_a, pltpu.roll(hx, 1, 1)),
            jnp.where(begin, seam_b, pltpu.roll(hz, 1, 1)),
        )

    def electric(z, hx_before, hz_before):
        hx, hy, hz = state[3, z + 1], state[4, z + 1], state[5, z + 1]
        loss, gain = coef[0, z], coef[1, z]
        state[0, z] = loss * state[0, z] + gain * ((hz - hz_before) - (hy - state[4, z]))
        state[1, z] = loss * state[1, z] + gain * (
            (hx - state[3, z]) - (hz - pltpu.roll(hz, 1, 0))
        )
        state[2, z] = loss * state[2, z] + gain * (
            (hy - pltpu.roll(hy, 1, 0)) - (hx - hx_before) - source
        )

    shifted, magnetics = {}, {}
    for t in range(Z + LAG_E + LAG_H):
        if t < Z:
            shifted[t] = shift_electric(t)
        if 0 <= t - LAG_E < Z:
            magnetics[t - LAG_E] = magnetic(t - LAG_E, *shifted.pop(t - LAG_E))
        if 0 <= t - LAG_E - LAG_H:
            electric(t - LAG_E - LAG_H, *magnetics.pop(t - LAG_E - LAG_H))


def steps(first, state, coef, seam, strips, edge_coefs, source, begin, strips_done):
    drives = drives_of(source)
    strips_step(first, strips, edge_coefs, seam, drives)
    begin()
    for s in range(first, K):
        if s + 1 < K:
            strips_step(s + 1, strips, edge_coefs, seam, drives)
        else:
            strips_done()
        sweep(s, state, coef, seam, source[:, :Y])


def load_fields(copies, e_hbm, h_hbm, loss_hbm, gain_hbm, halo_hbm, state, coef):
    for c in range(3):
        copies.start(e_hbm.at[c], state.at[c, pl.ds(0, Z), pl.ds(0, X)])
        copies.start(h_hbm.at[c], state.at[3 + c, pl.ds(1, Z), pl.ds(0, X)])
    copies.start(loss_hbm, coef.at[0, :, pl.ds(0, X)])
    copies.start(gain_hbm, coef.at[1, :, pl.ds(0, X)])
    for i in range(2):
        copies.start(halo_hbm.at[6 + i], coef.at[i, :, pl.ds(X, 8)])
    for c in range(3):
        state[c, Z] = jnp.zeros((24, Y), F32)
        state[3 + c, 0] = jnp.zeros((24, Y), F32)


def store_fields(copies, state, e_out, h_out):
    for c in range(3):
        copies.start(state.at[c, pl.ds(0, Z), pl.ds(0, X)], e_out.at[c])
        copies.start(state.at[3 + c, pl.ds(1, Z), pl.ds(0, X)], h_out.at[c])


def first_block(
    e_hbm, h_hbm, loss_hbm, gain_hbm, halo_hbm, source_hbm, cells_hbm, line_hbm, pack_hbm, even_hbm, odd_hbm,
    e_out, h_out, row_out, even_out, odd_out, strips_out, edge_coefs_out,
    state, coef, seam, strips, edge_coefs, source, cells, line, pack, sent, got, row, sems,
):
    fx, fy = lax.axis_index("fx"), lax.axis_index(("fy", "grp"))
    right, left = got.at[fy % 2], got.at[1 - fy % 2]
    up, down = sent.at[1 - fx % 2], sent.at[fx % 2]
    copies = Copies(sems)
    pairs = ((source_hbm, source), (cells_hbm, cells), (line_hbm, line), (pack_hbm, pack), (even_hbm, got.at[0]), (odd_hbm, got.at[1]))
    for origin, target in pairs:
        copies.start(origin, target)
    edges = copies.group()
    load_fields(copies, e_hbm, h_hbm, loss_hbm, gain_hbm, halo_hbm, state, coef)
    for c in range(6):
        copies.start(halo_hbm.at[c], state.at[c, pl.ds(c // 3, Z), pl.ds(X, 8)])
    fields = copies.group()
    copies.wait(edges)
    half = iota((24, Y), 1) % 16 < 8
    for c in range(8):
        low_ref, high_ref = (strips.at[c], strips.at[6 + c]) if c < 6 else (edge_coefs.at[c - 6], edge_coefs.at[c - 4])
        for part in range(4):
            at, pair = slice(Y * part, Y * part + Y), slice(Y * (part // 2), Y * (part // 2) + Y)
            own, from_left, from_right = pack[c, :, at], left[c, :, pair], right[c, :, pair]
            if part % 2:
                from_left = pltpu.roll(from_left, Y - 8, 1)
            else:
                from_right = pltpu.roll(from_right, 8, 1)
            low_ref[:, at] = jnp.where(half, from_left, own)
            high_ref[:, at] = jnp.where(half, own, from_right)
    copies.start(edge_coefs, edge_coefs_out)

    def pack_strips():
        copies.start(strips.at[:, pl.ds(0, X)], strips_out)
        low = iota((8, Y), 0) < 4
        for i in range(12):
            for j in range(2):
                a, b = (strips[i, :X, Y * k : Y * k + Y] for k in (j, j + 2))
                up[96 + 2 * i + j] = jnp.where(low, a[:8], pltpu.roll(b[:8], 4, 0))
                down[96 + 2 * i + j] = jnp.where(low, pltpu.roll(b[8:], 4, 0), a[8:])

    steps(
        0, state, coef, seam, strips, edge_coefs, source[...], lambda: copies.wait(fields), pack_strips
    )
    store_fields(copies, state, e_out, h_out)
    for c in range(6):
        pack_rows(lambda z: state[c, z + c // 3, :X], up, down, c)
    copies.start(sent.at[0], even_out)
    copies.start(sent.at[1], odd_out)
    mean = state[2, 0, :X]
    for z in range(1, Z):
        mean = mean + state[2, z, :X]
    row[...] = jnp.broadcast_to(line[...], row.shape)
    row[:, :SLOTS] = jnp.broadcast_to(port_means(mean * (1.0 / Z), cells[...]), (256, SLOTS))
    copies.start(row, row_out)
    copies.wait()


def second_block_start(
    e_hbm, h_hbm, loss_hbm, gain_hbm, halo_hbm, strips_hbm, edge_coefs_hbm, even_hbm, odd_hbm,
    state_out, coef_out, strips_out, state, coef, seam, strips, edge_coefs, got, sems,
):
    fx = lax.axis_index("fx")
    after, before = got.at[fx % 2], got.at[1 - fx % 2]
    copies = Copies(sems)
    pairs = ((even_hbm, got.at[0]), (odd_hbm, got.at[1]), (strips_hbm, strips.at[:, pl.ds(0, X)]), (edge_coefs_hbm, edge_coefs))
    for origin, target in pairs:
        copies.start(origin, target)
    edges = copies.group()
    load_fields(copies, e_hbm, h_hbm, loss_hbm, gain_hbm, halo_hbm, state, coef)
    fields = copies.group()
    copies.wait(edges)
    low = iota((8, Y), 0) < 4
    for c in range(6):
        for z in range(Z // 2):
            a, b = after[16 * c + z], before[16 * c + z]
            state[c, z + c // 3, X:] = jnp.where(low, a, b)
            state[c, z + Z // 2 + c // 3, X:] = pltpu.roll(jnp.where(low, b, a), 4, 0)
    for i in range(12):
        for j in range(2):
            a, b = after[96 + 2 * i + j], before[96 + 2 * i + j]
            strips[i, X:, Y * j : Y * j + Y] = jnp.where(low, a, b)
            strips[i, X:, Y * (j + 2) : Y * (j + 3)] = pltpu.roll(jnp.where(low, b, a), 4, 0)
    none = jnp.zeros((24, STRIP), F32)
    strips_step(0, strips, edge_coefs, seam, (none, none))
    copies.start(strips, strips_out)
    copies.wait(fields)
    copies.start(coef, coef_out)
    sweep(0, state, coef, seam, jnp.zeros((24, Y), F32))
    copies.start(state, state_out)
    copies.wait()


def second_block_end(
    state_hbm, coef_hbm, strips_hbm, edge_coefs_hbm, pick_hbm, mask_hbm, moved_hbm, inputs_hbm, gathered_hbm,
    e_out, h_out, state_out,
    state, coef, seam, strips, edge_coefs, pick, mask, moved, inputs, gathered, result, sems,
):
    copies = Copies(sems)
    pairs = ((gathered_hbm, gathered), (pick_hbm, pick), (mask_hbm, mask), (moved_hbm, moved), (inputs_hbm, inputs))
    for origin, target in pairs:
        copies.start(origin, target)
    ready = copies.group()
    for origin, target in ((strips_hbm, strips), (edge_coefs_hbm, edge_coefs), (coef_hbm, coef), (state_hbm, state)):
        copies.start(origin, target)
    fields = copies.group()
    copies.wait(ready)
    source, mine = port_sources(gathered, pick, mask)
    result[...] = moved[...] + input_part(inputs, mine)
    copies.start(result, state_out)
    copies.wait(fields)
    for z in range(Z):
        state[2, z] = state[2, z] - coef[1, z] * source[:, :Y]
    for i, drive in enumerate(drives_of(source)):
        strips[6 * i + 2] = strips[6 * i + 2] - edge_coefs[2 * i + 1] * drive
    steps(1, state, coef, seam, strips, edge_coefs, source, lambda: None, lambda: None)
    store_fields(copies, state, e_out, h_out)
    copies.wait()


def shape(*dims, dtype=F32):
    return jax.ShapeDtypeStruct(dims, dtype)


def call(kernel, outs, scratch, cost=1_000_000):
    scratch = [pltpu.VMEM(dims, F32) if isinstance(dims, tuple) else dims for dims in scratch]
    place = pl.BlockSpec(memory_space=pl.ANY)

    def run(*args):
        return pl.pallas_call(
            kernel,
            out_shape=outs,
            in_specs=[place] * len(args),
            out_specs=jax.tree.map(lambda _: place, outs),
            scratch_shapes=scratch + [pltpu.SemaphoreType.DMA((64,))],
            compiler_params=pltpu.CompilerParams(vmem_limit_bytes=56 * 1024 * 1024),
            cost_estimate=pl.CostEstimate(flops=cost, bytes_accessed=cost, transcendentals=0),
        )(*args)

    return run


def gate(values, received, other):
    def nothing(*refs):
        pass

    place = pl.BlockSpec(memory_space=pl.ANY)
    return pl.pallas_call(
        nothing,
        out_shape=[shape(*value.shape) for value in values],
        in_specs=[place] * (len(values) + 2),
        out_specs=[place] * len(values),
        input_output_aliases={i: i for i in range(len(values))},
    )(*values, received, other)


def neighbours(even, odd, axes, count):
    later = [(i, i + 1) for i in range(1, count - 1, 2)]
    return (
        lax.ppermute(even, axes, [(i, i ^ 1) for i in range(count)]),
        lax.ppermute(odd, axes, later + [(j, i) for i, j in later]),
    )


def exchange(row):
    return lax.all_to_all(row, ALL, 0, 0, tiled=True)


def body(
    efield, hfield, loss, gain, port_count, port_perm, port_cell,
    pole_state, transition, input_map, output_map, feedthrough,
):
    inputs = jnp.swapaxes(input_map, 1, 2)
    feed = jnp.transpose(feedthrough, (1, 2, 0))
    ints = functools.partial(pltpu.VMEM, dtype=I32)
    picks = 2 * LIST + LIST + 2 * MODELS
    tiles8, tiles6 = (128, 8, Y), (120, 8, Y)

    even, odd, row, fixed = call(
        first_kernel,
        (shape(*tiles8), shape(*tiles8), shape(256, Y), shape(1, Y)),
        [(8, Z, X, Y), (2, 2, MODELS), ints((1, SLOTS)), (MODELS, 256), (MODELS, 2, 256)]
        + [(2,) + tiles8, (8, Y), (256, Y), (1, Y)],
    )(efield, hfield, loss, gain, feed, port_cell, pole_state, output_map)
    even, odd = neighbours(even, odd, "fx", 8)
    gathered = exchange(row)
    ends = (8, 24, STRIP // 2)
    halo, pack, even, odd = call(
        side_kernel,
        (shape(8, Z, 8, Y), shape(8, 24, STRIP), shape(*ends), shape(*ends)),
        [(8, Z, X, Y), (2,) + tiles8, (8, Z, 8, Y), (8, 24, STRIP), (2,) + ends],
    )(efield, hfield, loss, gain, even, odd)
    moved = jnp.einsum("mpr,mr->mp", transition, pole_state, precision=HIGH)
    even, odd = gate((even, odd), gathered, moved)
    even, odd = neighbours(even, odd, ("fy", "grp"), 32)
    bits = pltpu.VMEM((picks, 256), jnp.bfloat16)
    pick, mask, source, state, line = call(
        index_kernel,
        (shape(picks, 256, dtype=jnp.bfloat16), shape(MASKS, Y), shape(24, 256), shape(MODELS, 256), shape(1, Y)),
        [ints((1, 256)), ints((32, Y)), (256, Y), (MODELS, 256), (MODELS, 2, 256), (MODELS, 2, 256), (1, Y)]
        + [bits, (MASKS, Y), (24, 256), (MODELS, 256), (1, Y)],
    )(port_count.reshape(1, 256), port_perm.reshape(32, Y), gathered, moved, inputs, output_map, fixed)

    fields, coefs, edges = (6, Z + 1, 24, Y), (2, Z, 24, Y), (12, 24, STRIP)
    scratch = [fields, coefs, (K, 2, 4, 24, Y), edges, (4, 24, STRIP)]
    outs = (shape(3, Z, X, Y), shape(3, Z, X, Y))
    electric, magnetic, row, next_even, next_odd, strips, edge_coefs = call(
        first_block,
        outs
        + (shape(256, Y), shape(*tiles6), shape(*tiles6), shape(12, X, STRIP), shape(4, 24, STRIP)),
        scratch
        + [(24, 256), ints((1, SLOTS)), (1, Y), (8, 24, STRIP), (2,) + tiles6, (2,) + ends, (256, Y)],
    )(efield, hfield, loss, gain, halo, source, port_cell, line, pack, even, odd)

    even, odd = neighbours(next_even, next_odd, "fx", 8)
    gathered = exchange(row)
    moved = jnp.einsum("mpr,mr->mp", transition, state, precision=HIGH)
    begun, coef, strips = call(
        second_block_start,
        (shape(*fields), shape(*coefs), shape(*edges)),
        scratch + [(2,) + tiles6],
    )(electric, magnetic, loss, gain, halo, strips, edge_coefs, even, odd)
    return call(
        second_block_end,
        outs + (shape(MODELS, 256),),
        scratch + [bits, (MASKS, Y), (MODELS, 256), (MODELS, 2, 256), (256, Y), (MODELS, 256)],
    )(begun, coef, strips, edge_coefs, pick, mask, moved, inputs, gathered)


def solution(mesh):
    return jax.shard_map(
        body,
        mesh=mesh,
        in_specs=(
            P(None, None, "fx", ("fy", "grp")),
            P(None, None, "fx", ("fy", "grp")),
            P(None, "fx", ("fy", "grp")),
            P(None, "fx", ("fy", "grp")),
            P(),
            P(),
            P(ALL, None),
            P(ALL, None),
            P(ALL, None, None),
            P(ALL, None, None),
            P(ALL, None, None),
            P(ALL, None, None),
        ),
        out_specs=(
            P(None, None, "fx", ("fy", "grp")),
            P(None, None, "fx", ("fy", "grp")),
            P(ALL, None),
        ),
        check_vma=False,
    )
```

profile of v0, /device:TPU:1, one launch (start us, length us, event | category | flops | bytes accessed | tf_op | source)
XLA Modules:
  0.0 87.6 jit_solution(1069113348836334174)
XLA Ops:
  0.6 0.0 copy-start
  0.6 0.0 copy-start.9
  0.7 3.1 %shard_map.139 = (f32[128,8,128]{2,1,0:T(8,128)}, f32[128,8,128]{2,1,0:T(8,128)}, f32[256,128]{1,0:T(8,128)}, f32[1,128]{1,0:T(1,128)}) custom-call(f32[3,32,16,128]{3,2,1,0:T(8,128)} %e_hbm.5, f32[3,32,16,128]{3,2,1,0:T(8,128)} %h_hbm.5, f32[32,16,128]{2,1,0:T(8,128)} %loss_hbm.7, f32[32,16,128]{2,1,0:T(8,128)} %gain_hbm.7, f32[2,2,8]{2,1,0:T(2,128)} %bitcast.35, ...), custom_call_target="tpu_custom_call" | custom-call | flops 1000000 | bytes 1000000 | tf_op jit(solution)/shard_map/pallas_call | solution.py:555
  3.8 2.6 %collective-permute-start = (f32[128,8,128]{2,1,0:T(8,128)}, f32[128,8,128]{2,1,0:T(8,128)S(1)}, u32[]{:S(2)}, u32[]{:S(2)}) collective-permute-start(f32[128,8,128]{2,1,0:T(8,128)} %get-tuple-element.28), channel_id=1, source_target_pairs={{0,32},{32,0},{64,96},{96,64},{128,160},{160,128},{192,224},{224,1... | collective-permute-start | bytes 1572872 | tf_op jit(solution)/shard_map/ppermute | solution.py:585
  6.3 0.7 collective-permute-start.1
  7.0 16.0 %all-to-all-start = ((f32[256,1,128]{2,1,0:T(1,128)}), f32[256,1,128]{2,1,0:T(1,128)S(1)}, u32[]{:S(2)}, u32[]{:S(2)}) async-start(f32[256,1,128]{2,1,0:T(1,128)} %bitcast.26), calls=%async_computation | async-start | bytes 262144 | tf_op jit(solution)/shard_map/all_to_all | solution.py:591
  23.0 0.0 copy-done
  23.0 0.0 copy-done.9
  23.0 1.8 %fusion.2 = f32[8,1,256]{2,1,0:T(1,128)S(1)} fusion(f32[8,256,256]{2,1,0:T(8,128)S(1)} %copy-done, f32[8,256,1]{1,0,2:T(8,128)S(1)} %bitcast.31), kind=kOutput, calls=%fused_computation.4 | convolution fusion | flops 6291456 | bytes 2113536 | tf_op jit(solution)/shard_map/mpr,mr->mp/dot_general | solution.py:618
  24.9 0.6 copy.30
  25.5 0.0 collective-permute-done.even_hbm
  25.5 0.0 copy-start.3
  25.5 0.0 collective-permute-done.1.odd_hbm
  25.5 0.8 copy-done.3
  26.3 0.0 copy-start.4
  26.3 0.8 copy-done.4
  27.1 4.2 %shard_map.140 = (f32[8,32,8,128]{3,2,1,0:T(8,128)}, f32[8,24,512]{2,1,0:T(8,128)}, f32[8,24,256]{2,1,0:T(8,128)}, f32[8,24,256]{2,1,0:T(8,128)}) custom-call(f32[3,32,16,128]{3,2,1,0:T(8,128)} %e_hbm.5, f32[3,32,16,128]{3,2,1,0:T(8,128)} %h_hbm.5, f32[32,16,128]{2,1,0:T(8,128)} %loss_hbm.7, f32[32,16,128]{2,1,0:T(8,128)} %gain_hbm.7, ...), custom_call_target="tpu_custom_call" | custom-call | flops 1000000 | bytes 1000000 | tf_op jit(solution)/shard_map/pallas_call | solution.py:555
  31.3 4.3 %all-to-all-done = f32[256,1,128]{2,1,0:T(1,128)S(1)} async-done(((f32[256,1,128]{2,1,0:T(1,128)}), f32[256,1,128]{2,1,0:T(1,128)S(1)}, u32[]{:S(2)}, u32[]{:S(2)}) %all-to-all-start) | async-done | bytes 131104 | tf_op jit(solution)/shard_map/all_to_all | solution.py:591
  35.7 0.0 copy-start.1
  35.7 0.7 copy-done.1
  36.3 0.5 collective-permute-start.2
  36.8 2.3 %collective-permute-start.3 = (f32[8,24,256]{2,1,0:T(8,128)}, f32[8,24,256]{2,1,0:T(8,128)S(1)}, u32[]{:S(2)}, u32[]{:S(2)}) collective-permute-start(f32[8,24,256]{2,1,0:T(8,128)} %get-tuple-element.39), channel_id=1, source_target_pairs={{1,2},{3,4},{5,6},{7,8},{9,10},{11,12},{13,14},{15,16},{17,18},{19... | collective-permute-start | bytes 589832 | tf_op jit(solution)/shard_map/ppermute | solution.py:586
  39.1 5.9 %shard_map.141 = (bf16[880,256]{1,0:T(8,128)(2,1)}, f32[1744,128]{1,0:T(8,128)}, f32[24,256]{1,0:T(8,128)}, f32[8,256]{1,0:T(8,128)}, f32[1,128]{1,0:T(1,128)}) custom-call(s32[1,256]{1,0:T(1,128)} %bitcast.36, s32[32,128]{1,0:T(8,128)} %bitcast.33, f32[256,128]{1,0:T(8,128)} %bitcast.23, f32[8,256]{1,0:T(8,128)} %bitcast.28, f32[8,2,256]{2,1,0:T(2,128)} %bitcast.29, ...), custom_call_target="tpu_custom_call" | custom-call | flops 1000000 | bytes 1000000 | tf_op jit(solution)/shard_map/pallas_call | solution.py:555
  45.0 0.0 collective-permute-done.2.even_hbm
  45.1 0.0 copy-start.7
  45.1 0.0 collective-permute-done.3.odd_hbm
  45.1 0.0 copy-start.8
  45.1 0.7 copy-done.7
  45.7 0.1 copy-done.8
  45.8 0.0 copy-start.10
  45.8 8.3 %shard_map.143 = (f32[3,32,16,128]{3,2,1,0:T(8,128)}, f32[3,32,16,128]{3,2,1,0:T(8,128)}, f32[256,128]{1,0:T(8,128)}, f32[120,8,128]{2,1,0:T(8,128)}, f32[120,8,...) custom-call(f32[3,32,16,128]{3,2,1,0:T(8,128)} %e_hbm.5, f32[3,32,16,128]{3,2,1,0:T(8,128)} %h_hbm.5, ...), custom_call_target="tpu_custom_call" | custom-call | flops 1000000 | bytes 1000000 | tf_op jit(solution)/shard_map/pallas_call | solution.py:555
  54.1 1.2 %collective-permute-start.4 = (f32[120,8,128]{2,1,0:T(8,128)}, f32[120,8,128]{2,1,0:T(8,128)S(1)}, u32[]{:S(2)}, u32[]{:S(2)}) collective-permute-start(f32[120,8,128]{2,1,0:T(8,128)} %get-tuple-element.44), channel_id=1, source_target_pairs={{0,32},{32,0},{64,96},{96,64},{128,160},{160,128},{192,224},{224,1... | collective-permute-start | bytes 1474568 | tf_op jit(solution)/shard_map/ppermute | solution.py:585
  55.4 0.7 collective-permute-start.5
  56.0 10.8 %all-to-all-start.1 = ((f32[256,1,128]{2,1,0:T(1,128)}), f32[256,1,128]{2,1,0:T(1,128)S(1)}, u32[]{:S(2)}, u32[]{:S(2)}) async-start(f32[256,1,128]{2,1,0:T(1,128)} %bitcast.25), calls=%async_computation.1 | async-start | bytes 262144 | tf_op jit(solution)/shard_map/all_to_all | solution.py:591
  66.9 0.0 copy-done.10
  66.9 1.8 %fusion = f32[8,1,256]{2,1,0:T(1,128)S(1)} fusion(f32[8,256,256]{2,1,0:T(8,128)S(1)} %copy-done, f32[8,256,1]{1,0,2:T(8,128)S(1)} %bitcast.34), kind=kOutput, calls=%fused_computation.1 | convolution fusion | flops 6291456 | bytes 2113536 | tf_op jit(solution)/shard_map/mpr,mr->mp/dot_general | solution.py:642
  68.7 0.6 copy.29
  69.3 0.0 collective-permute-done.4.even_hbm
  69.3 0.0 copy-start.5
  69.3 0.0 collective-permute-done.5.odd_hbm
  69.4 0.0 copy-start.6
  69.4 0.8 copy-done.5
  70.1 0.2 copy-done.6
  70.3 4.8 %shard_map.144 = (f32[6,33,24,128]{3,2,1,0:T(8,128)}, f32[2,32,24,128]{3,2,1,0:T(8,128)}, f32[12,24,512]{2,1,0:T(8,128)}) custom-call(f32[3,32,16,128]{3,2,1,0:T(8,128)} %get-tuple-element.40.e_hbm, f32[3,32,16,128]{3,2,1,0:T(8,128)} %get-tuple-element.41.h_hbm, f32[32,16,128]{2,1,0:T(8,128)} %loss_hbm.7, f32[32,16,128]{2,1,0:T(8,128)} %gain_hbm.7, ...), custom_call_target="tpu_custom_call" | custom-call | flops 1000000 | bytes 1000000 | tf_op jit(solution)/shard_map/pallas_call | solution.py:555
  75.1 4.0 %all-to-all-done.1 = f32[256,1,128]{2,1,0:T(1,128)S(1)} async-done(((f32[256,1,128]{2,1,0:T(1,128)}), f32[256,1,128]{2,1,0:T(1,128)S(1)}, u32[]{:S(2)}, u32[]{:S(2)}) %all-to-all-start.1) | async-done | bytes 131104 | tf_op jit(solution)/shard_map/all_to_all | solution.py:591
  79.2 0.0 copy-start.2
  79.2 0.7 copy-done.2
  79.8 7.6 %shard_map.145 = (f32[3,32,16,128]{3,2,1,0:T(8,128)}, f32[3,32,16,128]{3,2,1,0:T(8,128)}, f32[8,256]{1,0:T(8,128)}) custom-call(f32[6,33,24,128]{3,2,1,0:T(8,128)} %get-tuple-element.46.state_hbm, f32[2,32,24,128]{3,2,1,0:T(8,128)} %get-tuple-element.47.coef_hbm, f32[12,24,512]{2,1,0:T(8,128)} %get-tuple-element.48.strips_hbm, ...), custom_call_target="tpu_custom_call" | custom-call | flops 1000000 | bytes 1000000 | tf_op jit(solution)/shard_map/pallas_call | solution.py:555
  (1 shorter events, 0.0 us)
Async XLA Ops:
  0.6 22.4 %copy-start = (f32[8,256,256]{2,1,0:T(8,128)S(1)}, f32[8,256,256]{2,1,0:T(8,128)}, u32[]{:S(2)}) copy-start(f32[8,256,256]{2,1,0:T(8,128)} %param.20) | copy-start | bytes 6291460
  0.6 22.4 %copy-start.9 = (f32[8,256]{1,0:T(8,128)S(1)}, f32[8,256]{1,0:T(8,128)}, u32[]{:S(2)}) copy-start(f32[8,256]{1,0:T(8,128)} %state_hbm.1) | copy-start | bytes 24580
  3.8 21.7 %collective-permute-start = (f32[128,8,128]{2,1,0:T(8,128)}, f32[128,8,128]{2,1,0:T(8,128)S(1)}, u32[]{:S(2)}, u32[]{:S(2)}) collective-permute-start(f32[128,8,128]{2,1,0:T(8,128)} %get-tuple-element.28), channel_id=1, source_target_pairs={{0,32},{32,0},{64,96},{96,64},{128,160},{160,128},{192,224},{224,1... | collective-permute-start | bytes 1572872 | tf_op jit(solution)/shard_map/ppermute | solution.py:585
  6.3 19.2 %collective-permute-start.1 = (f32[128,8,128]{2,1,0:T(8,128)}, f32[128,8,128]{2,1,0:T(8,128)S(1)}, u32[]{:S(2)}, u32[]{:S(2)}) collective-permute-start(f32[128,8,128]{2,1,0:T(8,128)} %get-tuple-element.29), channel_id=1, source_target_pairs={{32,64},{96,128},{160,192},{64,32},{128,96},{192,160},{33,65},{97,... | collective-permute-start | bytes 1572872 | tf_op jit(solution)/shard_map/ppermute | solution.py:586
  7.0 28.6 %all-to-all-start = ((f32[256,1,128]{2,1,0:T(1,128)}), f32[256,1,128]{2,1,0:T(1,128)S(1)}, u32[]{:S(2)}, u32[]{:S(2)}) async-start(f32[256,1,128]{2,1,0:T(1,128)} %bitcast.26), calls=%async_computation | async-start | bytes 262144 | tf_op jit(solution)/shard_map/all_to_all | solution.py:591
  25.5 0.8 copy-start.3
  26.3 0.8 copy-start.4
  35.7 0.7 copy-start.1
  36.3 8.7 %collective-permute-start.2 = (f32[8,24,256]{2,1,0:T(8,128)}, f32[8,24,256]{2,1,0:T(8,128)S(1)}, u32[]{:S(2)}, u32[]{:S(2)}) collective-permute-start(f32[8,24,256]{2,1,0:T(8,128)} %get-tuple-element.38), channel_id=1, source_target_pairs={{0,1},{1,0},{2,3},{3,2},{4,5},{5,4},{6,7},{7,6},{8,9},{9,8},{10,11... | collective-permute-start | bytes 589832 | tf_op jit(solution)/shard_map/ppermute | solution.py:585
  36.8 8.3 %collective-permute-start.3 = (f32[8,24,256]{2,1,0:T(8,128)}, f32[8,24,256]{2,1,0:T(8,128)S(1)}, u32[]{:S(2)}, u32[]{:S(2)}) collective-permute-start(f32[8,24,256]{2,1,0:T(8,128)} %get-tuple-element.39), channel_id=1, source_target_pairs={{1,2},{3,4},{5,6},{7,8},{9,10},{11,12},{13,14},{15,16},{17,18},{19... | collective-permute-start | bytes 589832 | tf_op jit(solution)/shard_map/ppermute | solution.py:586
  45.1 0.7 copy-start.7
  45.1 0.7 copy-start.8
  45.8 21.1 %copy-start.10 = (f32[8,256]{1,0:T(8,128)S(1)}, f32[8,256]{1,0:T(8,128)}, u32[]{:S(2)}) copy-start(f32[8,256]{1,0:T(8,128)} %get-tuple-element.51) | copy-start | bytes 24580
  54.1 15.2 %collective-permute-start.4 = (f32[120,8,128]{2,1,0:T(8,128)}, f32[120,8,128]{2,1,0:T(8,128)S(1)}, u32[]{:S(2)}, u32[]{:S(2)}) collective-permute-start(f32[120,8,128]{2,1,0:T(8,128)} %get-tuple-element.44), channel_id=1, source_target_pairs={{0,32},{32,0},{64,96},{96,64},{128,160},{160,128},{192,224},{224,1... | collective-permute-start | bytes 1474568 | tf_op jit(solution)/shard_map/ppermute | solution.py:585
  55.4 14.0 %collective-permute-start.5 = (f32[120,8,128]{2,1,0:T(8,128)}, f32[120,8,128]{2,1,0:T(8,128)S(1)}, u32[]{:S(2)}, u32[]{:S(2)}) collective-permute-start(f32[120,8,128]{2,1,0:T(8,128)} %get-tuple-element.45), channel_id=1, source_target_pairs={{32,64},{96,128},{160,192},{64,32},{128,96},{192,160},{33,65},{97,... | collective-permute-start | bytes 1474568 | tf_op jit(solution)/shard_map/ppermute | solution.py:586
  56.0 23.1 %all-to-all-start.1 = ((f32[256,1,128]{2,1,0:T(1,128)}), f32[256,1,128]{2,1,0:T(1,128)S(1)}, u32[]{:S(2)}, u32[]{:S(2)}) async-start(f32[256,1,128]{2,1,0:T(1,128)} %bitcast.25), calls=%async_computation.1 | async-start | bytes 262144 | tf_op jit(solution)/shard_map/all_to_all | solution.py:591
  69.3 0.8 copy-start.5
  69.4 1.0 %copy-start.6 = (f32[120,8,128]{2,1,0:T(8,128)}, f32[120,8,128]{2,1,0:T(8,128)S(1)}, u32[]{:S(2)}) copy-start(f32[120,8,128]{2,1,0:T(8,128)S(1)} %collective-permute-done.5.odd_hbm) | copy-start | bytes 1474564
  79.2 0.7 copy-start.2
where the time goes:
time: 87.9 us; the launch traced here: 87.6 us
  starting transfers between devices  34.8 us (40%)
  Pallas kernels  34 us (39%)
  waiting for transfers between devices  8.36 us (10%)
  local copies, waits for them, and re-layouts  5.82 us (7%)
  matrix products  3.66 us (4%)
  between operations  0.99 us (1%)
    pallas_call x6, Pallas kernels, run(): pl.pallas_call(kernel, out_shape=outs, in_specs=[place] * len(args), out_...  34 us
    all_to_all x2, starting transfers between devices, exchange(): return lax.all_to_all(row, ALL, 0, 0, tiled=True)  26.8 us
    all_to_all x2, waiting for transfers between devices, exchange(): return lax.all_to_all(row, ALL, 0, 0, tiled=True)  8.35 us
    unnamed x22, local copies, waits for them, and re-layouts  4.58 us
    ppermute x3, starting transfers between devices, neighbours(): lax.ppermute(even, axes, [(i, i ^ 1) for i in range(count)])  4.3 us
    ppermute x3, starting transfers between devices, neighbours(): lax.ppermute(odd, axes, later + [(j, i) for i, j in later])  3.67 us
    dot_general x1, matrix products, body(): moved = jnp.einsum('mpr,mr->mp', transition, pole_state, precision=HIGH)  1.84 us
    dot_general x1, matrix products, body(): moved = jnp.einsum('mpr,mr->mp', transition, state, precision=HIGH)  1.82 us
  transfers between devices with their start and end apart: 8, of which 2 were waited for; matrix products, arithmetic and copies ran while one was open for 6% of the time, Pallas kernels for 17%

commit v1 on v0

--- a/solution.py
+++ b/solution.py
@@ -455,6 +455,10 @@
             high_ref[:, at] = jnp.where(half, own, from_right)
     copies.start(edge_coefs, edge_coefs_out)
 
+    def send(tiles):
+        copies.start(sent.at[0, tiles], even_out.at[tiles])
+        copies.start(sent.at[1, tiles], odd_out.at[tiles])
+
     def pack_strips():
         copies.start(strips.at[:, pl.ds(0, X)], strips_out)
         low = iota((8, Y), 0) < 4
@@ -463,21 +467,21 @@
                 a, b = (strips[i, :X, Y * k : Y * k + Y] for k in (j, j + 2))
                 up[96 + 2 * i + j] = jnp.where(low, a[:8], pltpu.roll(b[:8], 4, 0))
                 down[96 + 2 * i + j] = jnp.where(low, pltpu.roll(b[8:], 4, 0), a[8:])
+        send(pl.ds(96, 24))
 
     steps(
         0, state, coef, seam, strips, edge_coefs, source[...], lambda: copies.wait(fields), pack_strips
     )
     store_fields(copies, state, e_out, h_out)
-    for c in range(6):
-        pack_rows(lambda z: state[c, z + c // 3, :X], up, down, c)
-    copies.start(sent.at[0], even_out)
-    copies.start(sent.at[1], odd_out)
     mean = state[2, 0, :X]
     for z in range(1, Z):
         mean = mean + state[2, z, :X]
     row[...] = jnp.broadcast_to(line[...], row.shape)
     row[:, :SLOTS] = jnp.broadcast_to(port_means(mean * (1.0 / Z), cells[...]), (256, SLOTS))
     copies.start(row, row_out)
+    for c in range(6):
+        pack_rows(lambda z: state[c, z + c // 3, :X], up, down, c)
+        send(pl.ds(16 * c, 16))
     copies.wait()
 
 

time: 87.9 us -> 87.7 us (level)
  no operation moved by 1% of the time
where the time goes in v1:
time: 87.7 us; the launch traced here: 87.5 us
  starting transfers between devices  34.8 us (40%)
  Pallas kernels  33.8 us (39%)
  waiting for transfers between devices  8.36 us (10%)
  local copies, waits for them, and re-layouts  5.82 us (7%)
  matrix products  3.66 us (4%)
  between operations  0.99 us (1%)
    pallas_call x6, Pallas kernels, run(): pl.pallas_call(kernel, out_shape=outs, in_specs=[place] * len(args), out_...  33.8 us
    all_to_all x2, starting transfers between devices, exchange(): return lax.all_to_all(row, ALL, 0, 0, tiled=True)  26.8 us
    all_to_all x2, waiting for transfers between devices, exchange(): return lax.all_to_all(row, ALL, 0, 0, tiled=True)  8.35 us
    unnamed x22, local copies, waits for them, and re-layouts  4.58 us
    ppermute x3, starting transfers between devices, neighbours(): lax.ppermute(even, axes, [(i, i ^ 1) for i in range(count)])  4.3 us
    ppermute x3, starting transfers between devices, neighbours(): lax.ppermute(odd, axes, later + [(j, i) for i, j in later])  3.67 us
    dot_general x1, matrix products, body(): moved = jnp.einsum('mpr,mr->mp', transition, pole_state, precision=HIGH)  1.84 us
    dot_general x1, matrix products, body(): moved = jnp.einsum('mpr,mr->mp', transition, state, precision=HIGH)  1.82 us
  transfers between devices with their start and end apart: 8, of which 2 were waited for; matrix products, arithmetic and copies ran while one was open for 6% of the time, Pallas kernels for 17%

profile of v1, /device:TPU:1, one launch (start us, length us, event | category | flops | bytes accessed | tf_op | source)
XLA Modules:
  0.0 87.5 jit_solution(10769745605432824896)
XLA Ops:
  0.6 0.0 copy-start
  0.6 0.0 copy-start.9
  0.7 3.1 %shard_map.139 = (f32[128,8,128]{2,1,0:T(8,128)}, f32[128,8,128]{2,1,0:T(8,128)}, f32[256,128]{1,0:T(8,128)}, f32[1,128]{1,0:T(1,128)}) custom-call(f32[3,32,16,128]{3,2,1,0:T(8,128)} %e_hbm.5, f32[3,32,16,128]{3,2,1,0:T(8,128)} %h_hbm.5, f32[32,16,128]{2,1,0:T(8,128)} %loss_hbm.7, f32[32,16,128]{2,1,0:T(8,128)} %gain_hbm.7, f32[2,2,8]{2,1,0:T(2,128)} %bitcast.35, ...), custom_call_target="tpu_custom_call" | custom-call | flops 1000000 | bytes 1000000 | tf_op jit(solution)/shard_map/pallas_call | solution.py:559
  3.8 2.6 %collective-permute-start = (f32[128,8,128]{2,1,0:T(8,128)}, f32[128,8,128]{2,1,0:T(8,128)S(1)}, u32[]{:S(2)}, u32[]{:S(2)}) collective-permute-start(f32[128,8,128]{2,1,0:T(8,128)} %get-tuple-element.28), channel_id=1, source_target_pairs={{0,32},{32,0},{64,96},{96,64},{128,160},{160,128},{192,224},{224,1... | collective-permute-start | bytes 1572872 | tf_op jit(solution)/shard_map/ppermute | solution.py:589
  6.3 0.7 collective-permute-start.1
  7.0 16.0 %all-to-all-start = ((f32[256,1,128]{2,1,0:T(1,128)}), f32[256,1,128]{2,1,0:T(1,128)S(1)}, u32[]{:S(2)}, u32[]{:S(2)}) async-start(f32[256,1,128]{2,1,0:T(1,128)} %bitcast.26), calls=%async_computation | async-start | bytes 262144 | tf_op jit(solution)/shard_map/all_to_all | solution.py:595
  23.0 0.0 copy-done
  23.0 0.0 copy-done.9
  23.0 1.8 %fusion.2 = f32[8,1,256]{2,1,0:T(1,128)S(1)} fusion(f32[8,256,256]{2,1,0:T(8,128)S(1)} %copy-done, f32[8,256,1]{1,0,2:T(8,128)S(1)} %bitcast.31), kind=kOutput, calls=%fused_computation.4 | convolution fusion | flops 6291456 | bytes 2113536 | tf_op jit(solution)/shard_map/mpr,mr->mp/dot_general | solution.py:622
  24.9 0.6 copy.30
  25.5 0.0 collective-permute-done.even_hbm
  25.5 0.0 copy-start.3
  25.5 0.0 collective-permute-done.1.odd_hbm
  25.5 0.8 copy-done.3
  26.3 0.0 copy-start.4
  26.3 0.8 copy-done.4
  27.1 4.2 %shard_map.140 = (f32[8,32,8,128]{3,2,1,0:T(8,128)}, f32[8,24,512]{2,1,0:T(8,128)}, f32[8,24,256]{2,1,0:T(8,128)}, f32[8,24,256]{2,1,0:T(8,128)}) custom-call(f32[3,32,16,128]{3,2,1,0:T(8,128)} %e_hbm.5, f32[3,32,16,128]{3,2,1,0:T(8,128)} %h_hbm.5, f32[32,16,128]{2,1,0:T(8,128)} %loss_hbm.7, f32[32,16,128]{2,1,0:T(8,128)} %gain_hbm.7, ...), custom_call_target="tpu_custom_call" | custom-call | flops 1000000 | bytes 1000000 | tf_op jit(solution)/shard_map/pallas_call | solution.py:559
  31.3 4.3 %all-to-all-done = f32[256,1,128]{2,1,0:T(1,128)S(1)} async-done(((f32[256,1,128]{2,1,0:T(1,128)}), f32[256,1,128]{2,1,0:T(1,128)S(1)}, u32[]{:S(2)}, u32[]{:S(2)}) %all-to-all-start) | async-done | bytes 131104 | tf_op jit(solution)/shard_map/all_to_all | solution.py:595
  35.7 0.0 copy-start.1
  35.7 0.7 copy-done.1
  36.3 0.5 collective-permute-start.2
  36.8 2.3 %collective-permute-start.3 = (f32[8,24,256]{2,1,0:T(8,128)}, f32[8,24,256]{2,1,0:T(8,128)S(1)}, u32[]{:S(2)}, u32[]{:S(2)}) collective-permute-start(f32[8,24,256]{2,1,0:T(8,128)} %get-tuple-element.39), channel_id=1, source_target_pairs={{1,2},{3,4},{5,6},{7,8},{9,10},{11,12},{13,14},{15,16},{17,18},{19... | collective-permute-start | bytes 589832 | tf_op jit(solution)/shard_map/ppermute | solution.py:590
  39.1 5.9 %shard_map.141 = (bf16[880,256]{1,0:T(8,128)(2,1)}, f32[1744,128]{1,0:T(8,128)}, f32[24,256]{1,0:T(8,128)}, f32[8,256]{1,0:T(8,128)}, f32[1,128]{1,0:T(1,128)}) custom-call(s32[1,256]{1,0:T(1,128)} %bitcast.36, s32[32,128]{1,0:T(8,128)} %bitcast.33, f32[256,128]{1,0:T(8,128)} %bitcast.23, f32[8,256]{1,0:T(8,128)} %bitcast.28, f32[8,2,256]{2,1,0:T(2,128)} %bitcast.29, ...), custom_call_target="tpu_custom_call" | custom-call | flops 1000000 | bytes 1000000 | tf_op jit(solution)/shard_map/pallas_call | solution.py:559
  45.0 0.0 collective-permute-done.2.even_hbm
  45.1 0.0 copy-start.7
  45.1 0.0 collective-permute-done.3.odd_hbm
  45.1 0.0 copy-start.8
  45.1 0.7 copy-done.7
  45.7 0.1 copy-done.8
  45.8 0.0 copy-start.10
  45.8 8.2 %shard_map.143 = (f32[3,32,16,128]{3,2,1,0:T(8,128)}, f32[3,32,16,128]{3,2,1,0:T(8,128)}, f32[256,128]{1,0:T(8,128)}, f32[120,8,128]{2,1,0:T(8,128)}, f32[120,8,...) custom-call(f32[3,32,16,128]{3,2,1,0:T(8,128)} %e_hbm.5, f32[3,32,16,128]{3,2,1,0:T(8,128)} %h_hbm.5, ...), custom_call_target="tpu_custom_call" | custom-call | flops 1000000 | bytes 1000000 | tf_op jit(solution)/shard_map/pallas_call | solution.py:559
  54.0 1.2 %collective-permute-start.4 = (f32[120,8,128]{2,1,0:T(8,128)}, f32[120,8,128]{2,1,0:T(8,128)S(1)}, u32[]{:S(2)}, u32[]{:S(2)}) collective-permute-start(f32[120,8,128]{2,1,0:T(8,128)} %get-tuple-element.44), channel_id=1, source_target_pairs={{0,32},{32,0},{64,96},{96,64},{128,160},{160,128},{192,224},{224,1... | collective-permute-start | bytes 1474568 | tf_op jit(solution)/shard_map/ppermute | solution.py:589
  55.2 0.7 collective-permute-start.5
  55.9 10.8 %all-to-all-start.1 = ((f32[256,1,128]{2,1,0:T(1,128)}), f32[256,1,128]{2,1,0:T(1,128)S(1)}, u32[]{:S(2)}, u32[]{:S(2)}) async-start(f32[256,1,128]{2,1,0:T(1,128)} %bitcast.25), calls=%async_computation.1 | async-start | bytes 262144 | tf_op jit(solution)/shard_map/all_to_all | solution.py:595
  66.7 0.0 copy-done.10
  66.7 1.8 %fusion = f32[8,1,256]{2,1,0:T(1,128)S(1)} fusion(f32[8,256,256]{2,1,0:T(8,128)S(1)} %copy-done, f32[8,256,1]{1,0,2:T(8,128)S(1)} %bitcast.34), kind=kOutput, calls=%fused_computation.1 | convolution fusion | flops 6291456 | bytes 2113536 | tf_op jit(solution)/shard_map/mpr,mr->mp/dot_general | solution.py:646
  68.6 0.6 copy.29
  69.2 0.0 collective-permute-done.4.even_hbm
  69.2 0.0 copy-start.5
  69.2 0.0 collective-permute-done.5.odd_hbm
  69.2 0.0 copy-start.6
  69.2 0.8 copy-done.5
  70.0 0.2 copy-done.6
  70.2 4.8 %shard_map.144 = (f32[6,33,24,128]{3,2,1,0:T(8,128)}, f32[2,32,24,128]{3,2,1,0:T(8,128)}, f32[12,24,512]{2,1,0:T(8,128)}) custom-call(f32[3,32,16,128]{3,2,1,0:T(8,128)} %get-tuple-element.40.e_hbm, f32[3,32,16,128]{3,2,1,0:T(8,128)} %get-tuple-element.41.h_hbm, f32[32,16,128]{2,1,0:T(8,128)} %loss_hbm.7, f32[32,16,128]{2,1,0:T(8,128)} %gain_hbm.7, ...), custom_call_target="tpu_custom_call" | custom-call | flops 1000000 | bytes 1000000 | tf_op jit(solution)/shard_map/pallas_call | solution.py:559
  75.0 4.0 %all-to-all-done.1 = f32[256,1,128]{2,1,0:T(1,128)S(1)} async-done(((f32[256,1,128]{2,1,0:T(1,128)}), f32[256,1,128]{2,1,0:T(1,128)S(1)}, u32[]{:S(2)}, u32[]{:S(2)}) %all-to-all-start.1) | async-done | bytes 131104 | tf_op jit(solution)/shard_map/all_to_all | solution.py:595
  79.0 0.0 copy-start.2
  79.0 0.7 copy-done.2
  79.7 7.6 %shard_map.145 = (f32[3,32,16,128]{3,2,1,0:T(8,128)}, f32[3,32,16,128]{3,2,1,0:T(8,128)}, f32[8,256]{1,0:T(8,128)}) custom-call(f32[6,33,24,128]{3,2,1,0:T(8,128)} %get-tuple-element.46.state_hbm, f32[2,32,24,128]{3,2,1,0:T(8,128)} %get-tuple-element.47.coef_hbm, f32[12,24,512]{2,1,0:T(8,128)} %get-tuple-element.48.strips_hbm, ...), custom_call_target="tpu_custom_call" | custom-call | flops 1000000 | bytes 1000000 | tf_op jit(solution)/shard_map/pallas_call | solution.py:559
  (1 shorter events, 0.0 us)
Async XLA Ops:
  0.6 22.4 %copy-start = (f32[8,256,256]{2,1,0:T(8,128)S(1)}, f32[8,256,256]{2,1,0:T(8,128)}, u32[]{:S(2)}) copy-start(f32[8,256,256]{2,1,0:T(8,128)} %param.20) | copy-start | bytes 6291460
  0.6 22.4 %copy-start.9 = (f32[8,256]{1,0:T(8,128)S(1)}, f32[8,256]{1,0:T(8,128)}, u32[]{:S(2)}) copy-start(f32[8,256]{1,0:T(8,128)} %state_hbm.1) | copy-start | bytes 24580
  3.8 21.7 %collective-permute-start = (f32[128,8,128]{2,1,0:T(8,128)}, f32[128,8,128]{2,1,0:T(8,128)S(1)}, u32[]{:S(2)}, u32[]{:S(2)}) collective-permute-start(f32[128,8,128]{2,1,0:T(8,128)} %get-tuple-element.28), channel_id=1, source_target_pairs={{0,32},{32,0},{64,96},{96,64},{128,160},{160,128},{192,224},{224,1... | collective-permute-start | bytes 1572872 | tf_op jit(solution)/shard_map/ppermute | solution.py:589
  6.3 19.2 %collective-permute-start.1 = (f32[128,8,128]{2,1,0:T(8,128)}, f32[128,8,128]{2,1,0:T(8,128)S(1)}, u32[]{:S(2)}, u32[]{:S(2)}) collective-permute-start(f32[128,8,128]{2,1,0:T(8,128)} %get-tuple-element.29), channel_id=1, source_target_pairs={{32,64},{96,128},{160,192},{64,32},{128,96},{192,160},{33,65},{97,... | collective-permute-start | bytes 1572872 | tf_op jit(solution)/shard_map/ppermute | solution.py:590
  7.0 28.6 %all-to-all-start = ((f32[256,1,128]{2,1,0:T(1,128)}), f32[256,1,128]{2,1,0:T(1,128)S(1)}, u32[]{:S(2)}, u32[]{:S(2)}) async-start(f32[256,1,128]{2,1,0:T(1,128)} %bitcast.26), calls=%async_computation | async-start | bytes 262144 | tf_op jit(solution)/shard_map/all_to_all | solution.py:595
  25.5 0.8 copy-start.3
  26.3 0.8 copy-start.4
  35.7 0.7 copy-start.1
  36.3 8.7 %collective-permute-start.2 = (f32[8,24,256]{2,1,0:T(8,128)}, f32[8,24,256]{2,1,0:T(8,128)S(1)}, u32[]{:S(2)}, u32[]{:S(2)}) collective-permute-start(f32[8,24,256]{2,1,0:T(8,128)} %get-tuple-element.38), channel_id=1, source_target_pairs={{0,1},{1,0},{2,3},{3,2},{4,5},{5,4},{6,7},{7,6},{8,9},{9,8},{10,11... | collective-permute-start | bytes 589832 | tf_op jit(solution)/shard_map/ppermute | solution.py:589
  36.8 8.3 %collective-permute-start.3 = (f32[8,24,256]{2,1,0:T(8,128)}, f32[8,24,256]{2,1,0:T(8,128)S(1)}, u32[]{:S(2)}, u32[]{:S(2)}) collective-permute-start(f32[8,24,256]{2,1,0:T(8,128)} %get-tuple-element.39), channel_id=1, source_target_pairs={{1,2},{3,4},{5,6},{7,8},{9,10},{11,12},{13,14},{15,16},{17,18},{19... | collective-permute-start | bytes 589832 | tf_op jit(solution)/shard_map/ppermute | solution.py:590
  45.1 0.7 copy-start.7
  45.1 0.7 copy-start.8
  45.8 20.9 %copy-start.10 = (f32[8,256]{1,0:T(8,128)S(1)}, f32[8,256]{1,0:T(8,128)}, u32[]{:S(2)}) copy-start(f32[8,256]{1,0:T(8,128)} %get-tuple-element.51) | copy-start | bytes 24580
  54.0 15.2 %collective-permute-start.4 = (f32[120,8,128]{2,1,0:T(8,128)}, f32[120,8,128]{2,1,0:T(8,128)S(1)}, u32[]{:S(2)}, u32[]{:S(2)}) collective-permute-start(f32[120,8,128]{2,1,0:T(8,128)} %get-tuple-element.44), channel_id=1, source_target_pairs={{0,32},{32,0},{64,96},{96,64},{128,160},{160,128},{192,224},{224,1... | collective-permute-start | bytes 1474568 | tf_op jit(solution)/shard_map/ppermute | solution.py:589
  55.2 14.0 %collective-permute-start.5 = (f32[120,8,128]{2,1,0:T(8,128)}, f32[120,8,128]{2,1,0:T(8,128)S(1)}, u32[]{:S(2)}, u32[]{:S(2)}) collective-permute-start(f32[120,8,128]{2,1,0:T(8,128)} %get-tuple-element.45), channel_id=1, source_target_pairs={{32,64},{96,128},{160,192},{64,32},{128,96},{192,160},{33,65},{97,... | collective-permute-start | bytes 1474568 | tf_op jit(solution)/shard_map/ppermute | solution.py:590
  55.9 23.1 %all-to-all-start.1 = ((f32[256,1,128]{2,1,0:T(1,128)}), f32[256,1,128]{2,1,0:T(1,128)S(1)}, u32[]{:S(2)}, u32[]{:S(2)}) async-start(f32[256,1,128]{2,1,0:T(1,128)} %bitcast.25), calls=%async_computation.1 | async-start | bytes 262144 | tf_op jit(solution)/shard_map/all_to_all | solution.py:595
  69.2 0.8 copy-start.5
  69.2 1.0 %copy-start.6 = (f32[120,8,128]{2,1,0:T(8,128)}, f32[120,8,128]{2,1,0:T(8,128)S(1)}, u32[]{:S(2)}) copy-start(f32[120,8,128]{2,1,0:T(8,128)S(1)} %collective-permute-done.5.odd_hbm) | copy-start | bytes 1474564
  79.0 0.7 copy-start.2
